TPU v7x, 32 devices: a whole 2x2x4 slice. The times are simulated.
32 devices in a mesh: grp: 2 (over y), src: 16 (over z, x, core).
Axes of the slice: x: 2, y: 2, z: 4, core: 2. Of those that a mesh axis runs over, the one named last changes fastest.
Arguments:
- response: bfloat16 [2, 32, 512, 2048], P(None, ('grp', 'src')), parts along dimension 1, may hold values from -0.109335707 to 0.109335707, as said below
- direct_wave: bfloat16 [4096, 64, 1024], P(('grp', 'src')), parts along dimension 0, may hold values from -6 to 6
- onset: int32 [4096, 64], P(('grp', 'src')), parts along dimension 0, may hold values from 128 to 511
- band_start: int32 [2], P('grp'), parts along dimension 0, may hold values from 64 to 507
Outputs:
- focus_plus: bfloat16 [4096, 64, 1024], P(('grp', 'src')), parts along dimension 0
- focus_minus: bfloat16 [4096, 64, 1024], P(('grp', 'src')), parts along dimension 0
There are 2 independent parts, one for each index of `grp`. A program takes and returns all parts, laid end to end along the dimension named above; each array names one. Nothing has to cross between parts.
Inputs may be any that keep to these rules, and one draw needn't show every extreme that they name: For every frequency the response is symmetric in source and receiver: R[f, s, r] = R[f, r, s].
All inputs are finite; a program needn't handle non-finite values.
Results may differ from a plain program's by a relative error of at most 0.014.
Values may be sent and summed in bfloat16 or wider, within the bound.
A program may use at most 192 MiB of HBM per device.

v0:
```python
import math

import jax
import jax.numpy as jnp
from jax import lax
from jax.experimental import pallas as pl
from jax.experimental.pallas import tpu as pltpu
from jax.sharding import PartitionSpec as P

F32 = jnp.float32
BF16 = jnp.bfloat16
NT = (((1,), (1,)), ((), ()))


def table_rows(band_start, samples, freqs):
    times = jnp.arange(samples, dtype=jnp.int32)
    bins = band_start[0] + jnp.arange(freqs, dtype=jnp.int32)
    phase = bins[:, None] * times[None, :] % samples
    angle = phase.astype(F32) * (2.0 * math.pi / samples)
    both = jnp.stack([jnp.cos(angle), -jnp.sin(angle)], axis=1)
    return both.reshape(2 * freqs, samples).astype(BF16)


def forward_kernel(d_ref, t_ref, o_ref, out_ref, held):
    step = pl.program_id(0)
    count, focal, samples = d_ref.shape
    for pair in range(count // 2):
        rows = d_ref[2 * pair : 2 * pair + 2].reshape(2 * focal, samples)
        part = lax.dot_general(rows, t_ref[...], NT, preferred_element_type=F32)
        spot = pl.multiple_of((step * (count // 2) + pair) * 8, 8)
        held[pl.ds(spot, 8), :] = part.T[0:8, :]

    @pl.when(step == pl.num_programs(0) - 1)
    def _():
        for g in range(8):
            turned = held[pl.ds(g, 64, stride=8), :].T
            both = jnp.concatenate([turned[0:64], turned[64:128]], axis=1)
            out_ref[64 * g : 64 * g + 64, :] = both.astype(BF16)
        out_ref[512:640, :] = o_ref[...]


def exchange_kernel(
    m_ref, r_ref, t_ref, y_ref, w_ref,
    first, column, back, last, zsend, ysend, x0, onset, mix, products, pick, order, own,
    first_s, first_r, to_s, to_r, plane_s, plane_r, back_s, back_r, last_s, last_r,
):
    me = lax.axis_index("src")
    z = me // 4
    b = me % 4

    def in_plane(k):
        return z * 4 + (b + k) % 4

    def along(k):
        return ((z + k) % 4) * 4 + b

    def remote(src, dst, send, recv, device):
        return pltpu.make_async_remote_copy(
            src_ref=src, dst_ref=dst, send_sem=send, recv_sem=recv,
            device_id={"src": device}, device_id_type=pl.DeviceIdType.MESH,
        )

    barrier = pltpu.get_barrier_semaphore()
    for k in range(1, 4):
        for device in (in_plane(k), along(k)):
            pl.semaphore_signal(
                barrier, inc=1, device_id={"src": device}, device_id_type=pl.DeviceIdType.MESH
            )
    pl.semaphore_wait(barrier, 6)

    def first_copy(k):
        return remote(m_ref, first.at[b], first_s.at[k], first_r.at[k], in_plane(k))

    def to_copy(a, k):
        return remote(
            zsend.at[a, (z + k) % 4], column.at[a, z * 4 + b], to_s.at[a, k], to_r.at[a, k], along(k)
        )

    def plane_copy(a, kz, k):
        tile = ((z - kz + 4) % 4) * 4 + b
        return remote(
            column.at[a, tile], column.at[a, tile],
            plane_s.at[a, kz, k], plane_r.at[a, kz, k], in_plane(k),
        )

    def back_copy(a, k):
        return remote(
            ysend.at[a, (z + k) % 4], back.at[a, z], back_s.at[a, k], back_r.at[a, k], along(k)
        )

    def last_copy(e, k):
        return remote(back.at[2 + e], last.at[e, b], last_s.at[e, k], last_r.at[e, k], in_plane(k))

    for k in range(1, 4):
        first_copy(k).start()

    first[b] = m_ref[...]
    table = t_ref[...].astype(F32)
    for g in range(8):
        value = table[g : g + 1] * table
        high = value.astype(BF16)
        products[8 * g : 8 * g + 8, :] = high.astype(F32)
        products[64 + 8 * g : 72 + 8 * g, :] = (value - high.astype(F32))
    row = lax.broadcasted_iota(jnp.int32, (512, 128), 0)
    lane = lax.broadcasted_iota(jnp.int32, (512, 128), 1)
    station = (row // 128) * 128 + (row % 64) * 2 + (row % 128) // 64
    pick[...] = jnp.where(station == 4 * lane + b, 1.0, 0.0).astype(BF16)
    station = (row % 128) * 4 + row // 128
    own[...] = jnp.where(station == 128 * b + lane, 1.0, 0.0).astype(BF16)
    for part in range(4):
        order[:, 128 * part : 128 * part + 128] = jnp.where(
            station == 128 * part + lane, 1.0, 0.0
        ).astype(BF16)

    for k in range(1, 4):
        first_copy(k).wait_recv()
    gathered = jnp.concatenate([first[i] for i in range(4)], axis=1)
    picked = jnp.dot(gathered, pick[...], preferred_element_type=F32)
    x0[...] = picked[0:512]
    onset[...] = picked[512:576] * 4.0 + picked[576:640]
    for f in range(4):
        zsend[0, f] = picked[128 * f : 128 * f + 128].astype(BF16)

    def build_mix(a):
        begin = a * 512
        rows = products[:, pl.ds(pl.multiple_of(begin, 512), 512)].astype(BF16)
        times = lax.broadcasted_iota(jnp.int32, (512, 128), 0).astype(F32)
        times = jnp.where(a == 0, times, 512.0 - times)

        def body(p, carry):
            parts = []
            for q in range(2):
                limit = onset[pl.ds(2 * p + q, 1), :]
                parts.append(jnp.where(times < limit, 1.0, 0.0).astype(BF16))
            mask = jnp.concatenate(parts, axis=1)
            sums = jnp.dot(rows, mask, preferred_element_type=F32)
            sums = (sums[0:64] + sums[64:128]) * (1.0 / 512.0)
            for q in range(2):
                mix[a, pl.ds(2 * p + q, 64, stride=64), :] = sums[:, 128 * q : 128 * q + 128]
            return carry

        lax.fori_loop(0, 32, body, 0)

    def apply(a, carry):
        odd = a % 2
        sign = 1.0 - 2.0 * odd.astype(F32)
        for k in range(1, 4):
            to_copy(a, k).start()
        column[a, z * 4 + b] = zsend[a, z]
        for k in range(1, 4):
            plane_copy(a, 0, k).start()

        for kz in range(1, 4):
            to_copy(a, kz).wait_recv()
            for k in range(1, 4):
                plane_copy(a, kz, k).start()

        @pl.when(a < 2)
        def _():
            build_mix(a)

        real = jnp.zeros((128, 512), F32)
        imag = jnp.zeros((128, 512), F32)
        for kz in range(4):
            for k in range(1, 4):
                plane_copy(a, kz, k).wait_recv()
            chunk = (z - kz + 4) % 4
            tiles = jnp.concatenate([column[a, chunk * 4 + i] for i in range(4)], axis=1)
            ordered = jnp.dot(tiles, order[...], preferred_element_type=F32).astype(BF16)
            lanes = pl.ds(pl.multiple_of(chunk * 512, 512), 512)
            real += lax.dot_general(ordered, r_ref[0, :, lanes], NT, preferred_element_type=F32)
            imag += lax.dot_general(ordered, r_ref[1, :, lanes], NT, preferred_element_type=F32)
        top = (real[0:64] - sign * imag[64:128]).astype(BF16)
        low = (real[64:128] + sign * imag[0:64]).astype(BF16)
        for i in range(4):
            ysend[a, i, 0:64, :] = top[:, 128 * i : 128 * i + 128]
            ysend[a, i, 64:128, :] = low[:, 128 * i : 128 * i + 128]
        for k in range(1, 4):
            back_copy(a, k).start()
        back[a, z] = ysend[a, z]
        for k in range(1, 4):
            back_copy(a, k).wait_recv()

        @pl.when(a == 2)
        def _():
            for k in range(1, 4):
                last_copy(0, k).start()

        @pl.when(a < 3)
        def _():
            for q in range(4):
                spectra = []
                for f in range(4):
                    for c in range(2):
                        spectra.append(back[a, f, 64 * c + 16 * q : 64 * c + 16 * q + 16, :].astype(F32))
                for g in range(8):
                    base = x0[64 * g + 16 * q : 64 * g + 16 * q + 16, :]
                    total = jnp.where(odd == 1, base, 0.0)
                    for h in range(8):
                        spot = (8 * g + h) * 64 + 16 * q
                        total += mix[odd, spot : spot + 16, :] * spectra[h]
                    at = 64 * (g % 2) + 16 * q
                    zsend[a + 1, g // 2, at : at + 16, :] = total.astype(BF16)
        return carry

    lax.fori_loop(0, 4, apply, 0)

    for k in range(1, 4):
        last_copy(1, k).start()
    for e, out in ((0, y_ref), (1, w_ref)):
        for f in range(4):
            last[e, b, f] = back[2 + e, f]
        for k in range(1, 4):
            last_copy(e, k).wait_recv()
        for f in range(4):
            tiles = jnp.concatenate([last[e, i, f] for i in range(4)], axis=1)
            out[128 * f : 128 * f + 128, :] = jnp.dot(tiles, own[...], preferred_element_type=F32)

    for k in range(1, 4):
        first_copy(k).wait_send()
        last_copy(0, k).wait_send()
        last_copy(1, k).wait_send()

    def finish(a, carry):
        for k in range(1, 4):
            to_copy(a, k).wait_send()
            back_copy(a, k).wait_send()
            for kz in range(4):
                plane_copy(a, kz, k).wait_send()
        return carry

    lax.fori_loop(0, 4, finish, 0)


def output_kernel(d_ref, t_ref, o_ref, y_ref, w_ref, plus_ref, minus_ref, held):
    step = pl.program_id(0)
    count, focal, samples = d_ref.shape
    half = samples // 2

    @pl.when(step == 0)
    def _():
        for g in range(8):
            y = y_ref[64 * g : 64 * g + 64, :].T
            w = w_ref[64 * g : 64 * g + 64, :].T
            held[128 * g : 128 * g + 128, :] = jnp.concatenate([y, w], axis=1)
        limit = o_ref[...].astype(F32)
        held[1024:1152, :] = jnp.concatenate([limit, limit], axis=1)
        held[1152:2048, :] = jnp.zeros((896, 128), F32)

    times = lax.broadcasted_iota(jnp.int32, (focal, half), 1).astype(F32)
    scale = 2.0 / samples
    for i in range(count):
        rows = held[pl.ds(step * count + i, 16, stride=128), :]
        turned = jnp.concatenate([rows, jnp.zeros((112, 128), F32)], axis=0).T
        limit = turned[0:64, 8:9]
        left = turned.astype(BF16)
        y = jnp.dot(left[0:64], t_ref[:, 0:half], preferred_element_type=F32) * scale
        w = jnp.dot(left[64:128], t_ref[:, half:samples], preferred_element_type=F32) * scale
        minus_ref[i, :, 0:half] = jnp.where(times < limit, y, 0.0).astype(BF16)
        minus_ref[i, :, half:samples] = jnp.zeros((focal, half), BF16)
        plus_ref[i, :, 0:half] = d_ref[i, :, 0:half]
        kept = jnp.where(half - times < limit, w, 0.0)
        plus_ref[i, :, half:samples] = (d_ref[i, :, half:samples].astype(F32) + kept).astype(BF16)


def banded_shards(response, direct_wave, onset, band_start):
    owned, focal, samples = direct_wave.shape
    rows, stations = response.shape[2:]
    table = table_rows(band_start, samples, 4)
    padded = jnp.pad(table, ((0, 120), (0, 0)))
    turned = onset.reshape(64, 2, 64).transpose(2, 1, 0).reshape(64, 128)
    parts = jnp.concatenate([turned // 4, turned % 4], axis=0).astype(BF16)
    count = 8
    block = pl.BlockSpec((count, focal, samples), lambda i: (i, 0, 0))

    def whole(shape):
        return pl.BlockSpec(shape, lambda i: (0,) * len(shape))

    message = pl.pallas_call(
        forward_kernel,
        grid=(owned // count,),
        in_specs=[block, whole((128, samples)), whole((128, 128))],
        out_specs=whole((640, 128)),
        out_shape=jax.ShapeDtypeStruct((640, 128), BF16),
        scratch_shapes=[pltpu.VMEM((512, 128), F32)],
        compiler_params=pltpu.CompilerParams(vmem_limit_bytes=24 << 20),
    )(direct_wave, padded, parts)

    vmem = pl.BlockSpec(memory_space=pltpu.VMEM)
    dma = pltpu.SemaphoreType.DMA
    y, w = pl.pallas_call(
        exchange_kernel,
        in_specs=[vmem] * 3,
        out_specs=[vmem] * 2,
        out_shape=[jax.ShapeDtypeStruct((512, 128), F32)] * 2,
        scratch_shapes=[
            pltpu.VMEM((4, 640, 128), BF16),
            pltpu.VMEM((4, 16, 128, 128), BF16),
            pltpu.VMEM((4, 4, 128, 128), BF16),
            pltpu.VMEM((2, 4, 4, 128, 128), BF16),
            pltpu.VMEM((4, 4, 128, 128), BF16),
            pltpu.VMEM((4, 4, 128, 128), BF16),
            pltpu.VMEM((512, 128), F32),
            pltpu.VMEM((64, 128), F32),
            pltpu.VMEM((2, 4096, 128), F32),
            pltpu.VMEM((128, samples), F32),
            pltpu.VMEM((512, 128), BF16),
            pltpu.VMEM((512, 512), BF16),
            pltpu.VMEM((512, 128), BF16),
            dma((4,)), dma((4,)),
            dma((4, 4)), dma((4, 4)),
            dma((4, 4, 4)), dma((4, 4, 4)),
            dma((4, 4)), dma((4, 4)),
            dma((2, 4)), dma((2, 4)),
        ],
        compiler_params=pltpu.CompilerParams(
            collective_id=0, has_side_effects=True, vmem_limit_bytes=40 << 20
        ),
    )(message, response.reshape(2, rows, stations), table)

    return pl.pallas_call(
        output_kernel,
        grid=(owned // count,),
        in_specs=[block, whole((128, samples)), whole((128, 64)), whole((512, 128)), whole((512, 128))],
        out_specs=[block, block],
        out_shape=[jax.ShapeDtypeStruct(direct_wave.shape, BF16)] * 2,
        scratch_shapes=[pltpu.VMEM((2048, 128), F32)],
        compiler_params=pltpu.CompilerParams(vmem_limit_bytes=32 << 20),
    )(direct_wave, padded, onset, y, w)


ITERS = 2


def dft_tables(band_start, samples, freqs):
    times = jnp.arange(samples, dtype=jnp.int32)
    bins = band_start[0] + jnp.arange(freqs, dtype=jnp.int32)
    phase = times[:, None] * bins[None, :] % samples
    angle = phase.astype(jnp.float32) * (2.0 * math.pi / samples)
    cosine = jnp.cos(angle).astype(jnp.bfloat16)
    sine = jnp.sin(angle).astype(jnp.bfloat16)
    forward = jnp.concatenate([cosine, -sine], axis=1)
    backward = jnp.concatenate([cosine.T, -sine.T], axis=0)
    return (forward, backward)


def spectra_of(traces, forward):
    count, focal, samples = traces.shape
    freqs = forward.shape[1] // 2
    result = jnp.dot(
        traces.reshape(count * focal, samples), forward, preferred_element_type=jnp.float32
    )
    result = (
        result.reshape(count, focal, 2, freqs)
        .transpose(3, 0, 2, 1)
        .reshape(freqs, count, 2 * focal)
    )
    return result.astype(jnp.bfloat16)


def traces_of(spectra, backward):
    freqs, count, width = spectra.shape
    focal = width // 2
    samples = backward.shape[1]
    arranged = (
        spectra.reshape(freqs, count, 2, focal)
        .transpose(1, 3, 2, 0)
        .reshape(count * focal, 2 * freqs)
    )
    result = jnp.dot(arranged, backward, preferred_element_type=jnp.float32) * (2.0 / samples)
    return result.reshape(count, focal, samples)


def combine(real_term, imag_term, sign):
    half = real_term.shape[-1] // 2
    real_part = real_term[..., :half] - sign * imag_term[..., half:]
    imag_part = real_term[..., half:] + sign * imag_term[..., :half]
    return jnp.concatenate([real_part, imag_part], axis=-1)


def shards(response, direct_wave, onset, band_start):
    stations = response.shape[3]
    block_rows = response.shape[2]
    blocks = stations // block_rows
    devices = lax.axis_size("src")
    freqs = devices * response.shape[1] // blocks
    owned, focal, samples = direct_wave.shape
    share = owned // blocks
    forward, backward = dft_tables(band_start, samples, freqs)

    def apply_response(spectra, sign):
        copies = jnp.repeat(spectra, blocks, axis=0)
        column = lax.all_to_all(copies, "src", split_axis=0, concat_axis=1, tiled=True)
        real_term = jnp.einsum(
            "qjr,qrc->qjc", response[0], column, preferred_element_type=jnp.float32
        )
        imag_term = jnp.einsum(
            "qjr,qrc->qjc", response[1], column, preferred_element_type=jnp.float32
        )
        joined = combine(real_term, imag_term, sign).astype(jnp.bfloat16)
        returned = lax.all_to_all(joined, "src", split_axis=1, concat_axis=0, tiled=True)
        product = returned.reshape(freqs, blocks, share, 2 * focal).transpose(0, 2, 1, 3)
        return product.reshape(freqs, owned, 2 * focal)

    times = jnp.arange(samples, dtype=jnp.int32)
    keep_minus = times[None, None, :] < onset[:, :, None]
    keep_plus = (samples - times)[None, None, :] < onset[:, :, None]
    focus_plus = direct_wave
    focus_minus = direct_wave
    for step in range(ITERS):
        spectra = spectra_of(focus_plus, forward)
        product = apply_response(spectra, 1.0)
        traces = traces_of(product, backward)
        focus_minus = jnp.where(keep_minus, traces, 0.0).astype(jnp.bfloat16)
        spectra = spectra_of(focus_minus, forward)
        product = apply_response(spectra, -1.0)
        traces = traces_of(product, backward)
        focus_plus = (direct_wave.astype(jnp.float32) + jnp.where(keep_plus, traces, 0.0)).astype(
            jnp.bfloat16
        )
    return (focus_plus, focus_minus)


def solution(mesh):
    in_specs = (
        P(None, ("grp", "src"), None, None),
        P(("grp", "src"), None, None),
        P(("grp", "src"), None),
        P("grp"),
    )
    out_specs = (P(("grp", "src"), None, None), P(("grp", "src"), None, None))

    def body(response, direct_wave, onset, band_start):
        fits = (
            mesh.shape["src"] == 16
            and response.shape[1:] == (1, 512, 2048)
            and direct_wave.shape == (128, 64, 1024)
        )
        chosen = banded_shards if fits else shards
        return chosen(response, direct_wave, onset, band_start)

    return jax.shard_map(body, mesh=mesh, in_specs=in_specs, out_specs=out_specs, check_vma=False)
```

profile of v0, /device:TPU:0, one launch (start us, length us, event | category | flops | bytes accessed | tf_op | source)
XLA Modules:
  0.0 127.5 jit_solution(5973693516499139072)
XLA Ops:
  1.3 0.2 cosine_convert_fusion
  1.6 0.8 copy.14.o_ref
  2.4 0.1 copy.13
  2.5 0.1 reshape.116
  2.7 0.0 copy-start
  2.7 5.8 %copy-done = bf16[128,64,1024]{2,1,0:T(8,128)(2,1)S(1)} copy-done((bf16[128,64,1024]{2,1,0:T(8,128)(2,1)S(1)}, bf16[128,64,1024]{2,1,0:T(8,128)(2,1)}, u32[]{:S(2)}) %copy-start) | copy-done | bytes 16777240
  8.5 0.0 copy-start.2
  8.5 8.1 %shard_map.59.m_ref = bf16[640,128]{1,0:T(8,128)(2,1)S(1)} custom-call(bf16[128,64,1024]{2,1,0:T(8,128)(2,1)S(1)} %copy-done, bf16[128,1024]{1,0:T(8,128)(2,1)S(1)} %pad.4.t_ref, bf16[128,128]{1,0:T(8,128)(2,1)S(1)} %pad_maximum_fusion.o_ref), custom_call_target="tpu_custom_call" | custom-call | tf_op jit(solution)/shard_map/pallas_call | solution.py:279
  16.6 0.0 copy-done.2
  16.6 88.1 %shard_map.60 = (f32[512,128]{1,0:T(8,128)S(1)}, f32[512,128]{1,0:T(8,128)S(1)}) custom-call(bf16[640,128]{1,0:T(8,128)(2,1)S(1)} %shard_map.59.m_ref, bf16[2,512,2048]{2,1,0:T(8,128)(2,1)S(1)} %bitcast.6, bf16[8,1024]{1,0:T(8,128)(2,1)S(1)} %convert_element_type.21.t_ref), custom_call_target="tpu_custom_call" | custom-call | tf_op jit(solution)/shard_map/pallas_call | solution.py:291
  104.7 0.0 copy-start.1
  104.7 5.8 %copy-done.1 = bf16[128,64,1024]{2,1,0:T(8,128)(2,1)S(1)} copy-done((bf16[128,64,1024]{2,1,0:T(8,128)(2,1)S(1)}, bf16[128,64,1024]{2,1,0:T(8,128)(2,1)}, u32[]{:S(2)}) %copy-start.1) | copy-done | bytes 16777240
  110.5 17.1 %shard_map.61 = (bf16[128,64,1024]{2,1,0:T(8,128)(2,1)}, bf16[128,64,1024]{2,1,0:T(8,128)(2,1)}) custom-call(bf16[128,64,1024]{2,1,0:T(8,128)(2,1)S(1)} %copy-done.1, bf16[128,1024]{1,0:T(8,128)(2,1)S(1)} %pad.4.t_ref, s32[128,64]{1,0:T(8,128)S(1)} %copy.14.o_ref, f32[512,128]{1,0:T(8,128)S(1)} %get-tuple-element.4.y_ref, f32[512,128]{1,0:T(8,128)S(1)} %get-tuple-element.5.w_ref), custom_call_target="tpu_custom_call" | custom-call | tf_op jit(solution)/shard_map/pallas_call | solution.py:321
  (7 shorter events, 0.1 us)
Async XLA Ops:
  2.7 5.8 %copy-start = (bf16[128,64,1024]{2,1,0:T(8,128)(2,1)S(1)}, bf16[128,64,1024]{2,1,0:T(8,128)(2,1)}, u32[]{:S(2)}) copy-start(bf16[128,64,1024]{2,1,0:T(8,128)(2,1)} %d_ref.3) | copy-start | bytes 50331652
  8.5 8.1 %copy-start.2 = (bf16[2,1,512,2048]{3,2,1,0:T(8,128)(2,1)S(1)}, bf16[2,1,512,2048]{3,2,1,0:T(8,128)(2,1)}, u32[]{:S(2)}) copy-start(bf16[2,1,512,2048]{3,2,1,0:T(8,128)(2,1)} %param.4) | copy-start | bytes 12582916
  104.7 5.8 %copy-start.1 = (bf16[128,64,1024]{2,1,0:T(8,128)(2,1)S(1)}, bf16[128,64,1024]{2,1,0:T(8,128)(2,1)}, u32[]{:S(2)}) copy-start(bf16[128,64,1024]{2,1,0:T(8,128)(2,1)} %d_ref.3) | copy-start | bytes 50331652
where the time goes:
time: 128 us
  Pallas kernels  113 us (88%)
  local copies, waits for them, and re-layouts  12.6 us (10%)
  between operations  1.38 us (1%)
    pallas_call x1, Pallas kernels, banded_shards(): pl.pallas_call(exchange_kernel, in_specs=[vmem] * 3, out_specs=[vmem] * 2...  88.1 us
    pallas_call x1, Pallas kernels, banded_shards(): pl.pallas_call(output_kernel, grid=(owned // count,), in_specs=[block, wh...  17.1 us
    unnamed x7, local copies, waits for them, and re-layouts  12.4 us
    pallas_call x1, Pallas kernels, banded_shards(): pl.pallas_call(forward_kernel, grid=(owned // count,), in_specs=[block, w...  8.05 us

commit v1 on v0

--- a/solution.py
+++ b/solution.py
@@ -24,9 +24,10 @@
 def forward_kernel(d_ref, t_ref, o_ref, out_ref, held):
     step = pl.program_id(0)
     count, focal, samples = d_ref.shape
+    rows = d_ref[...].reshape(count * focal, samples)
+    parts = lax.dot_general(rows, t_ref[...], NT, preferred_element_type=F32)
     for pair in range(count // 2):
-        rows = d_ref[2 * pair : 2 * pair + 2].reshape(2 * focal, samples)
-        part = lax.dot_general(rows, t_ref[...], NT, preferred_element_type=F32)
+        part = parts[2 * focal * pair : 2 * focal * (pair + 1)]
         spot = pl.multiple_of((step * (count // 2) + pair) * 8, 8)
         held[pl.ds(spot, 8), :] = part.T[0:8, :]
 
@@ -41,12 +42,18 @@
 
 def exchange_kernel(
     m_ref, r_ref, t_ref, y_ref, w_ref,
-    first, column, back, last, zsend, ysend, x0, onset, mix, products, pick, order, own,
+    response, first, fsend, column, back, last, lsend, zsend, ysend, picked, onset, mix, products,
+    pick, order, split, own, load_s,
     first_s, first_r, to_s, to_r, plane_s, plane_r, back_s, back_r, last_s, last_r,
 ):
     me = lax.axis_index("src")
     z = me // 4
     b = me % 4
+
+    x = b // 2
+    core = b % 2
+    sibling = z * 4 + x * 2 + 1 - core
+    across = (1 - x) * 2 + core
 
     def in_plane(k):
         return z * 4 + (b + k) % 4
@@ -69,7 +76,9 @@
     pl.semaphore_wait(barrier, 6)
 
     def first_copy(k):
-        return remote(m_ref, first.at[b], first_s.at[k], first_r.at[k], in_plane(k))
+        return remote(
+            fsend.at[(b + k) % 4], first.at[b], first_s.at[k], first_r.at[k], in_plane(k)
+        )
 
     def to_copy(a, k):
         return remote(
@@ -77,10 +86,11 @@
         )
 
     def plane_copy(a, kz, k):
-        tile = ((z - kz + 4) % 4) * 4 + b
+        tile = ((z - kz + 4) % 4) * 4 + (across if k == 2 else b)
         return remote(
             column.at[a, tile], column.at[a, tile],
-            plane_s.at[a, kz, k], plane_r.at[a, kz, k], in_plane(k),
+            plane_s.at[a, kz, k], plane_r.at[a, kz, k],
+            z * 4 + across if k == 1 else sibling,
         )
 
     def back_copy(a, k):
@@ -89,39 +99,54 @@
         )
 
     def last_copy(e, k):
-        return remote(back.at[2 + e], last.at[e, b], last_s.at[e, k], last_r.at[e, k], in_plane(k))
-
+        return remote(
+            lsend.at[e, (b + k) % 4], last.at[e, b], last_s.at[e, k], last_r.at[e, k], in_plane(k)
+        )
+
+    load = pltpu.make_async_copy(r_ref, response, load_s)
+    load.start()
+
+    row = lax.broadcasted_iota(jnp.int32, (512, 128), 0)
+    lane = lax.broadcasted_iota(jnp.int32, (512, 128), 1)
+    quarter = row // 128
+    inner = row % 128
+
+    def ones(condition):
+        return jnp.where(condition, 1.0, 0.0).astype(BF16)
+
+    station = (inner % 64) * 2 + inner // 64
+    mine = jnp.concatenate([m_ref[160 * q : 160 * q + 160, :] for q in range(4)], axis=1)
+    for i in range(4):
+        chosen = ones((station == 4 * (lane % 32) + i) & (lane // 32 == quarter))
+        fsend[i] = jnp.dot(mine, chosen, preferred_element_type=F32).astype(BF16)
     for k in range(1, 4):
         first_copy(k).start()
-
-    first[b] = m_ref[...]
+    first[b] = fsend[b]
+
     table = t_ref[...].astype(F32)
     for g in range(8):
         value = table[g : g + 1] * table
-        high = value.astype(BF16)
-        products[8 * g : 8 * g + 8, :] = high.astype(F32)
-        products[64 + 8 * g : 72 + 8 * g, :] = (value - high.astype(F32))
-    row = lax.broadcasted_iota(jnp.int32, (512, 128), 0)
-    lane = lax.broadcasted_iota(jnp.int32, (512, 128), 1)
-    station = (row // 128) * 128 + (row % 64) * 2 + (row % 128) // 64
-    pick[...] = jnp.where(station == 4 * lane + b, 1.0, 0.0).astype(BF16)
-    station = (row % 128) * 4 + row // 128
-    own[...] = jnp.where(station == 128 * b + lane, 1.0, 0.0).astype(BF16)
-    for part in range(4):
-        order[:, 128 * part : 128 * part + 128] = jnp.where(
-            station == 128 * part + lane, 1.0, 0.0
-        ).astype(BF16)
+        high = value.astype(BF16).astype(F32)
+        products[8 * g : 8 * g + 8, :] = high
+        products[64 + 8 * g : 72 + 8 * g, :] = value - high
+    for i in range(4):
+        pick[i] = ones((lane == 32 * quarter + inner % 32) & (inner // 32 == i))
+        split[i] = ones((inner == 32 * i + lane % 32) & (lane // 32 == quarter))
+        own[i] = ones((lane == 4 * (inner % 32) + quarter) & (inner // 32 == i))
+        order[:, 128 * i : 128 * i + 128] = ones(inner * 4 + quarter == 128 * i + lane)
 
     for k in range(1, 4):
         first_copy(k).wait_recv()
     gathered = jnp.concatenate([first[i] for i in range(4)], axis=1)
-    picked = jnp.dot(gathered, pick[...], preferred_element_type=F32)
-    x0[...] = picked[0:512]
+    for i in range(4):
+        picked[160 * i : 160 * i + 160, :] = jnp.dot(
+            gathered, pick[i], preferred_element_type=F32
+        )
     onset[...] = picked[512:576] * 4.0 + picked[576:640]
     for f in range(4):
         zsend[0, f] = picked[128 * f : 128 * f + 128].astype(BF16)
 
-    def build_mix(a):
+    def build_mix(a, begin_p, end_p):
         begin = a * 512
         rows = products[:, pl.ds(pl.multiple_of(begin, 512), 512)].astype(BF16)
         times = lax.broadcasted_iota(jnp.int32, (512, 128), 0).astype(F32)
@@ -139,7 +164,7 @@
                 mix[a, pl.ds(2 * p + q, 64, stride=64), :] = sums[:, 128 * q : 128 * q + 128]
             return carry
 
-        lax.fori_loop(0, 32, body, 0)
+        lax.fori_loop(begin_p, end_p, body, 0)
 
     def apply(a, carry):
         odd = a % 2
@@ -147,29 +172,37 @@
         for k in range(1, 4):
             to_copy(a, k).start()
         column[a, z * 4 + b] = zsend[a, z]
-        for k in range(1, 4):
+        for k in range(2):
             plane_copy(a, 0, k).start()
 
         for kz in range(1, 4):
+            @pl.when(a < 2)
+            def _():
+                build_mix(a, (0, 10, 21, 32)[kz - 1], (0, 10, 21, 32)[kz])
+
             to_copy(a, kz).wait_recv()
-            for k in range(1, 4):
+            for k in range(2):
                 plane_copy(a, kz, k).start()
-
-        @pl.when(a < 2)
+            plane_copy(a, kz - 1, 1).wait_recv()
+            plane_copy(a, kz - 1, 2).start()
+        plane_copy(a, 3, 1).wait_recv()
+        plane_copy(a, 3, 2).start()
+
+        @pl.when(a == 0)
         def _():
-            build_mix(a)
+            load.wait()
 
         real = jnp.zeros((128, 512), F32)
         imag = jnp.zeros((128, 512), F32)
         for kz in range(4):
-            for k in range(1, 4):
-                plane_copy(a, kz, k).wait_recv()
+            plane_copy(a, kz, 0).wait_recv()
+            plane_copy(a, kz, 2).wait_recv()
             chunk = (z - kz + 4) % 4
             tiles = jnp.concatenate([column[a, chunk * 4 + i] for i in range(4)], axis=1)
             ordered = jnp.dot(tiles, order[...], preferred_element_type=F32).astype(BF16)
             lanes = pl.ds(pl.multiple_of(chunk * 512, 512), 512)
-            real += lax.dot_general(ordered, r_ref[0, :, lanes], NT, preferred_element_type=F32)
-            imag += lax.dot_general(ordered, r_ref[1, :, lanes], NT, preferred_element_type=F32)
+            real += lax.dot_general(ordered, response[0, :, lanes], NT, preferred_element_type=F32)
+            imag += lax.dot_general(ordered, response[1, :, lanes], NT, preferred_element_type=F32)
         top = (real[0:64] - sign * imag[64:128]).astype(BF16)
         low = (real[64:128] + sign * imag[0:64]).astype(BF16)
         for i in range(4):
@@ -181,6 +214,12 @@
         for k in range(1, 4):
             back_copy(a, k).wait_recv()
 
+        @pl.when(a >= 2)
+        def _():
+            tiles = jnp.concatenate([back[a, f] for f in range(4)], axis=1)
+            for i in range(4):
+                lsend[a - 2, i] = jnp.dot(tiles, split[i], preferred_element_type=F32).astype(BF16)
+
         @pl.when(a == 2)
         def _():
             for k in range(1, 4):
@@ -194,7 +233,7 @@
                     for c in range(2):
                         spectra.append(back[a, f, 64 * c + 16 * q : 64 * c + 16 * q + 16, :].astype(F32))
                 for g in range(8):
-                    base = x0[64 * g + 16 * q : 64 * g + 16 * q + 16, :]
+                    base = picked[64 * g + 16 * q : 64 * g + 16 * q + 16, :]
                     total = jnp.where(odd == 1, base, 0.0)
                     for h in range(8):
                         spot = (8 * g + h) * 64 + 16 * q
@@ -208,13 +247,12 @@
     for k in range(1, 4):
         last_copy(1, k).start()
     for e, out in ((0, y_ref), (1, w_ref)):
-        for f in range(4):
-            last[e, b, f] = back[2 + e, f]
+        last[e, b] = lsend[e, b]
         for k in range(1, 4):
             last_copy(e, k).wait_recv()
+        tiles = jnp.concatenate([last[e, i] for i in range(4)], axis=1)
         for f in range(4):
-            tiles = jnp.concatenate([last[e, i, f] for i in range(4)], axis=1)
-            out[128 * f : 128 * f + 128, :] = jnp.dot(tiles, own[...], preferred_element_type=F32)
+            out[128 * f : 128 * f + 128, :] = jnp.dot(tiles, own[f], preferred_element_type=F32)
 
     for k in range(1, 4):
         first_copy(k).wait_send()
@@ -226,7 +264,7 @@
             to_copy(a, k).wait_send()
             back_copy(a, k).wait_send()
             for kz in range(4):
-                plane_copy(a, kz, k).wait_send()
+                plane_copy(a, kz, k - 1).wait_send()
         return carry
 
     lax.fori_loop(0, 4, finish, 0)
@@ -283,30 +321,35 @@
         out_specs=whole((640, 128)),
         out_shape=jax.ShapeDtypeStruct((640, 128), BF16),
         scratch_shapes=[pltpu.VMEM((512, 128), F32)],
-        compiler_params=pltpu.CompilerParams(vmem_limit_bytes=24 << 20),
+        compiler_params=pltpu.CompilerParams(vmem_limit_bytes=56 << 20),
     )(direct_wave, padded, parts)
 
     vmem = pl.BlockSpec(memory_space=pltpu.VMEM)
     dma = pltpu.SemaphoreType.DMA
     y, w = pl.pallas_call(
         exchange_kernel,
-        in_specs=[vmem] * 3,
+        in_specs=[vmem, pl.BlockSpec(memory_space=pl.ANY), vmem],
         out_specs=[vmem] * 2,
         out_shape=[jax.ShapeDtypeStruct((512, 128), F32)] * 2,
         scratch_shapes=[
-            pltpu.VMEM((4, 640, 128), BF16),
+            pltpu.VMEM((2, rows, stations), BF16),
+            pltpu.VMEM((4, 160, 128), BF16),
+            pltpu.VMEM((4, 160, 128), BF16),
             pltpu.VMEM((4, 16, 128, 128), BF16),
             pltpu.VMEM((4, 4, 128, 128), BF16),
-            pltpu.VMEM((2, 4, 4, 128, 128), BF16),
+            pltpu.VMEM((2, 4, 128, 128), BF16),
+            pltpu.VMEM((2, 4, 128, 128), BF16),
             pltpu.VMEM((4, 4, 128, 128), BF16),
             pltpu.VMEM((4, 4, 128, 128), BF16),
-            pltpu.VMEM((512, 128), F32),
+            pltpu.VMEM((640, 128), F32),
             pltpu.VMEM((64, 128), F32),
             pltpu.VMEM((2, 4096, 128), F32),
             pltpu.VMEM((128, samples), F32),
-            pltpu.VMEM((512, 128), BF16),
+            pltpu.VMEM((4, 512, 128), BF16),
             pltpu.VMEM((512, 512), BF16),
-            pltpu.VMEM((512, 128), BF16),
+            pltpu.VMEM((4, 512, 128), BF16),
+            pltpu.VMEM((4, 512, 128), BF16),
+            dma,
             dma((4,)), dma((4,)),
             dma((4, 4)), dma((4, 4)),
             dma((4, 4, 4)), dma((4, 4, 4)),
@@ -325,7 +368,7 @@
         out_specs=[block, block],
         out_shape=[jax.ShapeDtypeStruct(direct_wave.shape, BF16)] * 2,
         scratch_shapes=[pltpu.VMEM((2048, 128), F32)],
-        compiler_params=pltpu.CompilerParams(vmem_limit_bytes=32 << 20),
+        compiler_params=pltpu.CompilerParams(vmem_limit_bytes=56 << 20),
     )(direct_wave, padded, onset, y, w)
 
 

time: 128 us -> 133 us (1.039)
  Pallas kernels: 113 us -> 125 us
  local copies, waits for them, and re-layouts: 12.6 us -> 4.11 us
    unnamed x7 -> x11, local copies, waits for them, and re-layouts: 12.4 us -> 3.16 us
    pallas_call x1, Pallas kernels: 8.05 us -> 15.6 us  [banded_shards(): pl.pallas_call(forward_kernel, grid=(owned // count,), in_specs=[block, w...]
    pallas_call x1, Pallas kernels: 17.1 us -> 24.5 us  [banded_shards(): pl.pallas_call(output_kernel, grid=(owned // count,), in_specs=[block, wh...]
    pallas_call x1, Pallas kernels: 88.1 us -> 85.3 us  [banded_shards(): pl.pallas_call(exchange_kernel, in_specs=[vmem, pl.BlockSpec(memory_space...]
where the time goes in v1:
time: 133 us; the launch traced here: 132 us
  Pallas kernels  125 us (94%)
  local copies, waits for them, and re-layouts  4.11 us (3%)
  between operations  1.35 us (1%)
    pallas_call x1, Pallas kernels, banded_shards(): pl.pallas_call(exchange_kernel, in_specs=[vmem, pl.BlockSpec(memory_space...  85.3 us
    pallas_call x1, Pallas kernels, banded_shards(): pl.pallas_call(output_kernel, grid=(owned // count,), in_specs=[block, wh...  24.5 us
    pallas_call x1, Pallas kernels, banded_shards(): pl.pallas_call(forward_kernel, grid=(owned // count,), in_specs=[block, w...  15.6 us
    unnamed x11, local copies, waits for them, and re-layouts  3.16 us

profile of v1, /device:TPU:0, one launch (start us, length us, event | category | flops | bytes accessed | tf_op | source)
XLA Modules:
  0.0 131.7 jit_solution(7487652270419327491)
XLA Ops:
  1.3 0.2 cosine_convert_fusion
  1.6 0.8 copy.14.o_ref
  2.4 0.0 copy-start.4
  2.4 0.1 copy.13
  2.5 0.1 reshape.116
  2.6 0.0 copy-start
  2.7 0.6 pad_maximum_fusion.o_ref
  3.3 0.7 pad.4.t_ref
  4.0 15.6 %shard_map.59.m_ref = bf16[640,128]{1,0:T(8,128)(2,1)} custom-call(bf16[128,64,1024]{2,1,0:T(8,128)(2,1)} %d_ref.3, bf16[128,1024]{1,0:T(8,128)(2,1)} %pad.4.t_ref, bf16[128,128]{1,0:T(8,128)(2,1)} %pad_maximum_fusion.o_ref), custom_call_target="tpu_custom_call" | custom-call | tf_op jit(solution)/shard_map/pallas_call | solution.py:317
  19.7 0.0 copy-done
  19.7 0.0 copy-start.1
  19.7 0.9 copy-done.1
  20.6 85.3 %shard_map.60 = (f32[512,128]{1,0:T(8,128)S(1)}, f32[512,128]{1,0:T(8,128)S(1)}) custom-call(bf16[640,128]{1,0:T(8,128)(2,1)S(1)} %copy-done.1, bf16[2,512,2048]{2,1,0:T(8,128)(2,1)S(1)} %bitcast.6, bf16[8,1024]{1,0:T(8,128)(2,1)S(1)} %convert_element_type.21.t_ref), custom_call_target="tpu_custom_call" | custom-call | tf_op jit(solution)/shard_map/pallas_call | solution.py:329
  105.9 0.0 copy-start.2
  105.9 0.7 copy-done.2
  106.6 0.0 copy-start.3
  106.6 0.7 copy-done.3
  107.3 0.0 copy-done.4
  107.3 24.5 %shard_map.61 = (bf16[128,64,1024]{2,1,0:T(8,128)(2,1)}, bf16[128,64,1024]{2,1,0:T(8,128)(2,1)}) custom-call(bf16[128,64,1024]{2,1,0:T(8,128)(2,1)} %d_ref.3, bf16[128,1024]{1,0:T(8,128)(2,1)} %pad.4.t_ref, s32[128,64]{1,0:T(8,128)} %copy-done.4, f32[512,128]{1,0:T(8,128)} %copy-done.2, f32[512,128]{1,0:T(8,128)} %copy-done.3), custom_call_target="tpu_custom_call" | custom-call | tf_op jit(solution)/shard_map/pallas_call | solution.py:364
  (5 shorter events, 0.1 us)
Async XLA Ops:
  2.4 104.8 %copy-start.4 = (s32[128,64]{1,0:T(8,128)}, s32[128,64]{1,0:T(8,128)S(1)}, u32[]{:S(2)}) copy-start(s32[128,64]{1,0:T(8,128)S(1)} %copy.14.o_ref) | copy-start | bytes 98308
  2.6 17.0 %copy-start = (bf16[2,1,512,2048]{3,2,1,0:T(8,128)(2,1)S(1)}, bf16[2,1,512,2048]{3,2,1,0:T(8,128)(2,1)}, u32[]{:S(2)}) copy-start(bf16[2,1,512,2048]{3,2,1,0:T(8,128)(2,1)} %param.4) | copy-start | bytes 12582916
  19.7 0.9 copy-start.1
  105.9 0.7 copy-start.2
  106.6 0.7 copy-start.3

commit v2 on v1

--- a/solution.py
+++ b/solution.py
@@ -21,15 +21,21 @@
     return both.reshape(2 * freqs, samples).astype(BF16)
 
 
-def forward_kernel(d_ref, t_ref, o_ref, out_ref, held):
+def forward_kernel(d0_ref, d1_ref, d2_ref, d3_ref, t_ref, o_ref, out_ref, held, columns):
     step = pl.program_id(0)
-    count, focal, samples = d_ref.shape
-    rows = d_ref[...].reshape(count * focal, samples)
-    parts = lax.dot_general(rows, t_ref[...], NT, preferred_element_type=F32)
-    for pair in range(count // 2):
-        part = parts[2 * focal * pair : 2 * focal * (pair + 1)]
-        spot = pl.multiple_of((step * (count // 2) + pair) * 8, 8)
-        held[pl.ds(spot, 8), :] = part.T[0:8, :]
+    pieces = (d0_ref, d1_ref, d2_ref, d3_ref)
+    count, focal, samples = d0_ref.shape
+    @pl.when(step == 0)
+    def _():
+        columns[...] = t_ref[...].astype(F32).T.astype(BF16)
+
+    for piece in range(4):
+        rows = pieces[piece][...].reshape(count * focal, samples)
+        parts = jnp.dot(rows, columns[...], preferred_element_type=F32)
+        for pair in range(count // 2):
+            part = parts[2 * focal * pair : 2 * focal * (pair + 1)]
+            spot = ((step * 4 + piece) * (count // 2) + pair) * 8
+            held[pl.ds(pl.multiple_of(spot, 8), 8), :] = part.T[0:8, :]
 
     @pl.when(step == pl.num_programs(0) - 1)
     def _():
@@ -270,10 +276,29 @@
     lax.fori_loop(0, 4, finish, 0)
 
 
-def output_kernel(d_ref, t_ref, o_ref, y_ref, w_ref, plus_ref, minus_ref, held):
+def output_kernel(d_ref, t_ref, o_ref, y_ref, w_ref, plus_out, minus_out, held, plus_ref, minus_ref, sent, ys, ws):
     step = pl.program_id(0)
     count, focal, samples = d_ref.shape
     half = samples // 2
+    slot = step % 2
+
+    def copies(at):
+        found = []
+        for n, (source, target) in enumerate(((plus_ref, plus_out), (minus_ref, minus_out))):
+            for part in range(4):
+                found.append(
+                    pltpu.make_async_copy(
+                        source.at[at % 2, pl.ds(2 * part, 2)],
+                        target.at[pl.ds(at * count + 2 * part, 2)],
+                        sent.at[n, at % 2, part],
+                    )
+                )
+        return found
+
+    @pl.when(step >= 2)
+    def _():
+        for copy in copies(step - 2):
+            copy.wait()
 
     @pl.when(step == 0)
     def _():
@@ -286,19 +311,34 @@
         held[1152:2048, :] = jnp.zeros((896, 128), F32)
 
     times = lax.broadcasted_iota(jnp.int32, (focal, half), 1).astype(F32)
-    scale = 2.0 / samples
+    limits, lefts = [], []
     for i in range(count):
         rows = held[pl.ds(step * count + i, 16, stride=128), :]
         turned = jnp.concatenate([rows, jnp.zeros((112, 128), F32)], axis=0).T
-        limit = turned[0:64, 8:9]
-        left = turned.astype(BF16)
-        y = jnp.dot(left[0:64], t_ref[:, 0:half], preferred_element_type=F32) * scale
-        w = jnp.dot(left[64:128], t_ref[:, half:samples], preferred_element_type=F32) * scale
-        minus_ref[i, :, 0:half] = jnp.where(times < limit, y, 0.0).astype(BF16)
-        minus_ref[i, :, half:samples] = jnp.zeros((focal, half), BF16)
-        plus_ref[i, :, 0:half] = d_ref[i, :, 0:half]
+        limits.append(turned[0:64, 8:9])
+        lefts.append(turned.astype(BF16))
+    left = jnp.concatenate([each[0:64] for each in lefts], axis=0)
+    ys[...] = jnp.dot(left, t_ref[:, 0:half], preferred_element_type=F32)
+    left = jnp.concatenate([each[64:128] for each in lefts], axis=0)
+    ws[...] = jnp.dot(left, t_ref[:, half:samples], preferred_element_type=F32)
+    for i in range(count):
+        limit = limits[i]
+        y = ys[64 * i : 64 * i + 64, :]
+        w = ws[64 * i : 64 * i + 64, :]
+        minus_ref[slot, i, :, 0:half] = jnp.where(times < limit, y, 0.0).astype(BF16)
+        minus_ref[slot, i, :, half:samples] = jnp.zeros((focal, half), BF16)
+        plus_ref[slot, i, :, 0:half] = d_ref[i, :, 0:half]
         kept = jnp.where(half - times < limit, w, 0.0)
-        plus_ref[i, :, half:samples] = (d_ref[i, :, half:samples].astype(F32) + kept).astype(BF16)
+        plus_ref[slot, i, :, half:samples] = (d_ref[i, :, half:samples].astype(F32) + kept).astype(BF16)
+
+    for copy in copies(step):
+        copy.start()
+
+    @pl.when(step == pl.num_programs(0) - 1)
+    def _():
+        for at in (step - 1, step):
+            for copy in copies(at):
+                copy.wait()
 
 
 def banded_shards(response, direct_wave, onset, band_start):
@@ -316,13 +356,16 @@
 
     message = pl.pallas_call(
         forward_kernel,
-        grid=(owned // count,),
-        in_specs=[block, whole((128, samples)), whole((128, 128))],
+        grid=(owned // 16,),
+        in_specs=[
+            pl.BlockSpec((4, focal, samples), lambda i, j=j: (4 * i + j, 0, 0)) for j in range(4)
+        ]
+        + [whole((128, samples)), whole((128, 128))],
         out_specs=whole((640, 128)),
         out_shape=jax.ShapeDtypeStruct((640, 128), BF16),
-        scratch_shapes=[pltpu.VMEM((512, 128), F32)],
+        scratch_shapes=[pltpu.VMEM((512, 128), F32), pltpu.VMEM((samples, 128), BF16)],
         compiler_params=pltpu.CompilerParams(vmem_limit_bytes=56 << 20),
-    )(direct_wave, padded, parts)
+    )(direct_wave, direct_wave, direct_wave, direct_wave, padded, parts)
 
     vmem = pl.BlockSpec(memory_space=pltpu.VMEM)
     dma = pltpu.SemaphoreType.DMA
@@ -357,7 +400,10 @@
             dma((2, 4)), dma((2, 4)),
         ],
         compiler_params=pltpu.CompilerParams(
-            collective_id=0, has_side_effects=True, vmem_limit_bytes=40 << 20
+            collective_id=0, has_side_effects=True, vmem_limit_bytes=24 << 20
+        ),
+        cost_estimate=pl.CostEstimate(
+            flops=1 << 33, bytes_accessed=192 << 20, transcendentals=0
         ),
     )(message, response.reshape(2, rows, stations), table)
 
@@ -365,11 +411,18 @@
         output_kernel,
         grid=(owned // count,),
         in_specs=[block, whole((128, samples)), whole((128, 64)), whole((512, 128)), whole((512, 128))],
-        out_specs=[block, block],
+        out_specs=[pl.BlockSpec(memory_space=pl.ANY)] * 2,
         out_shape=[jax.ShapeDtypeStruct(direct_wave.shape, BF16)] * 2,
-        scratch_shapes=[pltpu.VMEM((2048, 128), F32)],
-        compiler_params=pltpu.CompilerParams(vmem_limit_bytes=56 << 20),
-    )(direct_wave, padded, onset, y, w)
+        scratch_shapes=[
+            pltpu.VMEM((2048, 128), F32),
+            pltpu.VMEM((2, count, focal, samples), BF16),
+            pltpu.VMEM((2, count, focal, samples), BF16),
+            dma((2, 2, 4)),
+            pltpu.VMEM((count * focal, samples // 2), F32),
+            pltpu.VMEM((count * focal, samples // 2), F32),
+        ],
+        compiler_params=pltpu.CompilerParams(vmem_limit_bytes=20 << 20),
+    )(direct_wave, padded * (2.0 / samples), onset, y, w)
 
 
 ITERS = 2

time: 133 us -> 124 us (0.932)
  Pallas kernels: 125 us -> 113 us
  local copies, waits for them, and re-layouts: 4.11 us -> 7.76 us
    pallas_call x1, Pallas kernels: 24.5 us -> 16 us  [banded_shards(): pl.pallas_call(output_kernel, grid=(owned // count,), in_specs=[block, wh...]
    unnamed x11 -> x7, local copies, waits for them, and re-layouts: 3.16 us -> 7.53 us
    pallas_call x1, Pallas kernels: 15.6 us -> 11.7 us  [banded_shards(): pl.pallas_call(forward_kernel, grid=(owned // 16,), in_specs=[pl.BlockSpe...]
where the time goes in v2:
time: 124 us
  Pallas kernels  113 us (91%)
  local copies, waits for them, and re-layouts  7.76 us (6%)
  other arithmetic  1.65 us (1%)
  between operations  1.35 us (1%)
    pallas_call x1, Pallas kernels, banded_shards(): pl.pallas_call(exchange_kernel, in_specs=[vmem, pl.BlockSpec(memory_space...  85.3 us
    pallas_call x1, Pallas kernels, banded_shards(): pl.pallas_call(output_kernel, grid=(owned // count,), in_specs=[block, wh...  16 us
    pallas_call x1, Pallas kernels, banded_shards(): pl.pallas_call(forward_kernel, grid=(owned // 16,), in_specs=[pl.BlockSpe...  11.7 us
    unnamed x7, local copies, waits for them, and re-layouts  7.53 us

profile of v2, /device:TPU:0, one launch (start us, length us, event | category | flops | bytes accessed | tf_op | source)
XLA Modules:
  0.0 123.8 jit_solution(11281035059057982846)
XLA Ops:
  1.3 0.2 cosine_convert_fusion
  1.6 0.8 copy.14.o_ref
  2.4 0.1 copy.13
  2.5 0.1 reshape.116
  2.7 0.6 pad_maximum_fusion.o_ref
  3.3 0.8 fusion.7
  4.0 0.0 copy-start.2
  4.1 11.7 %shard_map.59.m_ref = bf16[640,128]{1,0:T(8,128)(2,1)} custom-call(bf16[128,64,1024]{2,1,0:T(8,128)(2,1)} %d_ref.1, bf16[128,64,1024]{2,1,0:T(8,128)(2,1)} %d_ref.1, bf16[128,64,1024]{2,1,0:T(8,128)(2,1)} %d_ref.1, bf16[128,64,1024]{2,1,0:T(8,128)(2,1)} %d_ref.1, bf16[128,1024]{1,0:T(8,128)(2,1)} %get-tuple-element.8.t_ref, ...), custom_call_target="tpu_custom_call" | custom-call | tf_op jit(solution)/shard_map/pallas_call | solution.py:357
  15.8 0.0 copy-done.2
  15.8 0.0 copy-start.1
  15.8 0.9 copy-done.1
  16.7 85.3 %shard_map.60 = (f32[512,128]{1,0:T(8,128)S(1)}, f32[512,128]{1,0:T(8,128)S(1)}) custom-call(bf16[640,128]{1,0:T(8,128)(2,1)S(1)} %copy-done.1, bf16[2,512,2048]{2,1,0:T(8,128)(2,1)S(1)} %bitcast.7, bf16[8,1024]{1,0:T(8,128)(2,1)S(1)} %convert_element_type.21.t_ref), custom_call_target="tpu_custom_call" | custom-call | flops 8589934592 | bytes 201326592 | tf_op jit(solution)/shard_map/pallas_call | solution.py:372
  102.0 0.0 copy-start
  102.0 5.8 %copy-done = bf16[128,64,1024]{2,1,0:T(8,128)(2,1)S(1)} copy-done((bf16[128,64,1024]{2,1,0:T(8,128)(2,1)S(1)}, bf16[128,64,1024]{2,1,0:T(8,128)(2,1)}, u32[]{:S(2)}) %copy-start) | copy-done | bytes 16777240
  107.8 16.0 %shard_map.61 = (bf16[128,64,1024]{2,1,0:T(8,128)(2,1)}, bf16[128,64,1024]{2,1,0:T(8,128)(2,1)}) custom-call(bf16[128,64,1024]{2,1,0:T(8,128)(2,1)S(1)} %copy-done, bf16[128,1024]{1,0:T(8,128)(2,1)S(1)} %get-tuple-element.9.t_ref, s32[128,64]{1,0:T(8,128)S(1)} %copy.14.o_ref, f32[512,128]{1,0:T(8,128)S(1)} %get-tuple-element.4.y_ref, ...), custom_call_target="tpu_custom_call" | custom-call | tf_op jit(solution)/shard_map/pallas_call | solution.py:410
  (5 shorter events, 0.1 us)
Async XLA Ops:
  4.0 11.7 %copy-start.2 = (bf16[2,1,512,2048]{3,2,1,0:T(8,128)(2,1)S(1)}, bf16[2,1,512,2048]{3,2,1,0:T(8,128)(2,1)}, u32[]{:S(2)}) copy-start(bf16[2,1,512,2048]{3,2,1,0:T(8,128)(2,1)} %param.4) | copy-start | bytes 12582916
  15.8 0.9 copy-start.1
  102.0 5.8 %copy-start = (bf16[128,64,1024]{2,1,0:T(8,128)(2,1)S(1)}, bf16[128,64,1024]{2,1,0:T(8,128)(2,1)}, u32[]{:S(2)}) copy-start(bf16[128,64,1024]{2,1,0:T(8,128)(2,1)} %d_ref.1) | copy-start | bytes 50331652
